TPU v7x, 32 devices: a whole 2x2x4 slice. The times are simulated.
32 devices in a mesh: dp: 16 (over z, y, core), seq: 2 (over x).
Axes of the slice: x: 2, y: 2, z: 4, core: 2. Of those that a mesh axis runs over, the one named last changes fastest.
Arguments:
- inputs: bfloat16 [16, 1024, 768], P('dp', 'seq'), may hold values from -6 to 6
- modality: int32 [16, 1024], P('dp'), may hold values from 0 to 2, never falling along the last dimension, each value on 1 to 512 neighbouring positions
- key_valid_mask: int32 [16, 1024], P('dp'), may hold values 0 or 1
- output_gradient: bfloat16 [16, 1024, 768], P('dp', 'seq'), may hold values from -6 to 6
- mats: float32 [768, 9216], P('dp'), may hold values from -2 to 2
- mats_momentum: float32 [768, 9216], P('dp')
- mats_average: float32 [768, 9216], P('dp'), may hold values from -2 to 2
- smalls: float32 [768, 15], P('dp'), may hold values from -2 to 2
- smalls_momentum: float32 [768, 15], P('dp')
- smalls_average: float32 [768, 15], P('dp'), may hold values from -2 to 2
Outputs:
- block_out: bfloat16 [16, 1024, 768], P('dp', 'seq')
- input_grad: bfloat16 [16, 1024, 768], P('dp', 'seq')
- mats_grad: float32 [768, 9216], P('dp')
- new_mats: float32 [768, 9216], P('dp')
- new_mats_momentum: float32 [768, 9216], P('dp')
- new_mats_average: float32 [768, 9216], P('dp')
- smalls_grad: float32 [768, 15], P('dp')
- out_bias_grad: float32 [768], P('dp')
- new_smalls: float32 [768, 15], P('dp')
- new_smalls_momentum: float32 [768, 15], P('dp')
- new_smalls_average: float32 [768, 15], P('dp')
Inputs may be any that keep to these rules, and one draw needn't show every extreme that they name: Along a document's positions the modality never falls; each of the three fills 1 to 512 positions, one of them exactly that many.
All inputs are finite; a program needn't handle non-finite values. No bound on the sum of `key_valid_mask` on one device may be relied on, other than what follows from the above.
Results may differ from a plain program's by a relative error of at most 0.019.
Values may be sent and summed in bfloat16 or wider, within the bound.
No kernel may reach another device: no remote copies, remote signals or barrier semaphores. Data moves between devices by JAX's collectives and lax.ppermute only.
A program may use at most 192 MiB of HBM per device.

v0:
```python
import math
import jax
import jax.numpy as jnp
from jax import lax
from jax.sharding import PartitionSpec as P

MODEL_WIDTH = 768
H = 12
HD = 64
FF = 3072
epsilon = 1e-06
momentum_rate = 0.9
decay_rate = 0.0001
average_rate = 0.75
base_rate = 0.03
masked_score = -1e30


def product(left, right):
    return jnp.dot(left, right, preferred_element_type=jnp.float32)


def product_tn(left, right):
    return lax.dot_general(
        left, right, (((0,), (0,)), ((), ())), preferred_element_type=jnp.float32
    )


def product_nt(left, right):
    return lax.dot_general(
        left, right, (((1,), (1,)), ((), ())), preferred_element_type=jnp.float32
    )


def normalize(rows, gain, shift):
    mean = jnp.mean(rows, axis=-1, keepdims=True)
    centred = rows - mean
    spread = jnp.mean(centred * centred, axis=-1, keepdims=True)
    return centred * lax.rsqrt(spread + epsilon) * gain + shift


def exact_gelu(values):
    return jax.nn.gelu(values, approximate=False)


def head_scores(query_heads, key_heads, live_doc):
    scores = (
        jnp.einsum("qhe,khe->hqk", query_heads, key_heads, preferred_element_type=jnp.float32)
        * 0.125
    )
    return jnp.where(live_doc[None, None, :] > 0, scores, masked_score)


def attention_forward_pass(item):
    query_doc, keys_doc, values_doc, live_doc = item
    query_heads = query_doc.reshape(query_doc.shape[0], H, HD)
    key_heads = keys_doc.reshape(keys_doc.shape[0], H, HD)
    value_heads = values_doc.reshape(values_doc.shape[0], H, HD)
    scores = head_scores(query_heads, key_heads, live_doc)
    top = jnp.max(scores, axis=-1, keepdims=True)
    expd = jnp.exp(scores - top)
    total = jnp.sum(expd, axis=-1, keepdims=True)
    prob = (expd / total).astype(jnp.bfloat16)
    attention_output = jnp.einsum(
        "hqk,khe->qhe", prob, value_heads, preferred_element_type=jnp.float32
    )
    return (attention_output.reshape(query_doc.shape[0], H * HD), (top + jnp.log(total))[..., 0])


def attention_backward_pass(item):
    query_doc, keys_doc, values_doc, live_doc, log_sum_normalizer, grad_doc = item
    element_count = query_doc.shape[0]
    length = keys_doc.shape[0]
    query_heads = query_doc.reshape(element_count, H, HD)
    key_heads = keys_doc.reshape(length, H, HD)
    value_heads = values_doc.reshape(length, H, HD)
    grad_heads = grad_doc.reshape(element_count, H, HD)
    scores = head_scores(query_heads, key_heads, live_doc)
    prob = jnp.exp(scores - log_sum_normalizer[..., None])
    grad_prob = jnp.einsum(
        "qhe,khe->hqk", grad_heads, value_heads, preferred_element_type=jnp.float32
    )
    grad_values = jnp.einsum(
        "hqk,qhe->khe", prob.astype(jnp.bfloat16), grad_heads, preferred_element_type=jnp.float32
    )
    inner = jnp.sum(prob * grad_prob, axis=-1, keepdims=True)
    grad_scores = (prob * (grad_prob - inner)).astype(jnp.bfloat16)
    grad_query = (
        jnp.einsum("hqk,khe->qhe", grad_scores, key_heads, preferred_element_type=jnp.float32)
        * 0.125
    )
    grad_keys = (
        jnp.einsum("hqk,qhe->khe", grad_scores, query_heads, preferred_element_type=jnp.float32)
        * 0.125
    )
    return (
        grad_query.reshape(element_count, H * HD),
        grad_keys.reshape(length, H * HD),
        grad_values.reshape(length, H * HD),
    )


def per_device(
    inputs,
    modality,
    key_valid_mask,
    output_gradient,
    mats,
    mats_momentum,
    mats_average,
    smalls,
    smalls_momentum,
    smalls_average,
):
    docs, local_len, width = inputs.shape
    seq_len = modality.shape[1]
    rows = docs * local_len
    low_mats = mats.astype(jnp.bfloat16)
    w_qkv, w_out, w_up, w_down, whole_smalls = (
        lax.all_gather(low_mats[:, 0 : 3 * MODEL_WIDTH], "dp", axis=0, tiled=True),
        lax.all_gather(low_mats[:, 3 * MODEL_WIDTH : 4 * MODEL_WIDTH], "dp", axis=0, tiled=True),
        lax.all_gather(
            low_mats[:, 4 * MODEL_WIDTH : 4 * MODEL_WIDTH + FF], "dp", axis=0, tiled=True
        ),
        lax.all_gather(low_mats[:, 4 * MODEL_WIDTH + FF :], "dp", axis=0, tiled=True),
        lax.all_gather(smalls.astype(jnp.bfloat16), "dp", axis=0, tiled=True),
    )
    params = whole_smalls.astype(jnp.float32)
    bias_qkv = jnp.concatenate([params[:, 0], jnp.zeros_like(params[:, 0]), params[:, 1]])
    bias_up = jnp.transpose(params[:, 8:12]).reshape(FF)
    embed = jnp.transpose(whole_smalls[:, 12:15])
    leading_key = (jnp.arange(seq_len) == 0).astype(jnp.int32)
    valid_positions = jnp.maximum(key_valid_mask, leading_key[None, :])
    local_start = lax.axis_index("seq") * local_len
    local_modality = lax.dynamic_slice_in_dim(modality, local_start, local_len, 1)
    onehot = (
        local_modality.reshape(rows)[:, None] == jnp.arange(3, dtype=jnp.int32)[None, :]
    ).astype(jnp.bfloat16)
    x_in = inputs.reshape(rows, width).astype(jnp.float32) + product(onehot, embed)
    x_low = x_in.astype(jnp.bfloat16)
    qkv = (product(x_low, w_qkv) + bias_qkv).astype(jnp.bfloat16)
    query_documents = qkv[:, 0:width].reshape(docs, local_len, width)
    keys_local = qkv[:, width : 2 * width].reshape(docs, local_len, width)
    values_local = qkv[:, 2 * width :].reshape(docs, local_len, width)
    every_key, every_value = (
        lax.all_gather(keys_local, "seq", axis=1, tiled=True),
        lax.all_gather(values_local, "seq", axis=1, tiled=True),
    )
    attention_output, log_sum_normalizer = lax.map(
        attention_forward_pass, (query_documents, every_key, every_value, valid_positions)
    )
    out_low = attention_output.reshape(rows, width).astype(jnp.bfloat16)
    mixed = product(out_low, w_out) + params[:, 2]
    first_in = x_in + mixed
    first = normalize(first_in, params[:, 4], params[:, 5])
    first_low = first.astype(jnp.bfloat16)
    up = product(first_low, w_up) + bias_up
    act_low = exact_gelu(up).astype(jnp.bfloat16)
    ffo = product_nt(act_low, w_down) + params[:, 3]
    second_in = first + ffo
    result = normalize(second_in, params[:, 6], params[:, 7])
    block_out = result.astype(jnp.bfloat16).reshape(docs, local_len, width)
    w_qkv, w_out, w_up, w_down = (
        lax.all_gather(low_mats[:, 0 : 3 * MODEL_WIDTH], "dp", axis=0, tiled=True),
        lax.all_gather(low_mats[:, 3 * MODEL_WIDTH : 4 * MODEL_WIDTH], "dp", axis=0, tiled=True),
        lax.all_gather(
            low_mats[:, 4 * MODEL_WIDTH : 4 * MODEL_WIDTH + FF], "dp", axis=0, tiled=True
        ),
        lax.all_gather(low_mats[:, 4 * MODEL_WIDTH + FF :], "dp", axis=0, tiled=True),
    )
    grad_rows = output_gradient.reshape(rows, width).astype(jnp.float32)
    second_out, second_pull = jax.vjp(normalize, second_in, params[:, 6], params[:, 7])
    grad_second, grad_gain2, grad_shift2 = second_pull(grad_rows)
    grad_ffo = grad_second.astype(jnp.bfloat16)
    grad_bias_down = jnp.sum(grad_ffo.astype(jnp.float32), axis=0)
    grad_w_down = product_tn(grad_ffo, act_low)
    grad_act = product(grad_ffo, w_down)
    gelu_out, gelu_pull = jax.vjp(exact_gelu, up)
    grad_up = gelu_pull(grad_act)[0].astype(jnp.bfloat16)
    grad_bias_up = jnp.sum(grad_up.astype(jnp.float32), axis=0)
    grad_w_up = product_tn(first_low, grad_up)
    grad_first = grad_second + product_nt(grad_up, w_up)
    first_out, first_pull = jax.vjp(normalize, first_in, params[:, 4], params[:, 5])
    grad_first_in, grad_gain1, grad_shift1 = first_pull(grad_first)
    grad_mixed = grad_first_in.astype(jnp.bfloat16)
    grad_bias_out = jnp.sum(grad_mixed.astype(jnp.float32), axis=0)
    grad_w_out = product_tn(out_low, grad_mixed)
    grad_out = product_nt(grad_mixed, w_out).astype(jnp.bfloat16)
    output_gradient_documents = grad_out.reshape(docs, local_len, width)
    grad_query, grad_keys_all, grad_values_all = lax.map(
        attention_backward_pass,
        (
            query_documents,
            every_key,
            every_value,
            valid_positions,
            log_sum_normalizer,
            output_gradient_documents,
        ),
    )
    grad_keys, grad_values = (
        lax.psum_scatter(
            grad_keys_all.astype(jnp.bfloat16), "seq", scatter_dimension=1, tiled=True
        ).astype(jnp.float32),
        lax.psum_scatter(
            grad_values_all.astype(jnp.bfloat16), "seq", scatter_dimension=1, tiled=True
        ).astype(jnp.float32),
    )
    grad_qkv = jnp.concatenate(
        [
            grad_query.reshape(rows, width).astype(jnp.bfloat16),
            grad_keys.reshape(rows, width).astype(jnp.bfloat16),
            grad_values.reshape(rows, width).astype(jnp.bfloat16),
        ],
        axis=1,
    )
    grad_bias_qkv = jnp.sum(grad_qkv.astype(jnp.float32), axis=0)
    grad_w_qkv = product_tn(x_low, grad_qkv)
    grad_x_in = grad_first_in + product_nt(grad_qkv, w_qkv)
    grad_embed = lax.dot_general(
        onehot.astype(jnp.float32),
        grad_x_in,
        (((0,), (0,)), ((), ())),
        precision=lax.Precision.HIGHEST,
        preferred_element_type=jnp.float32,
    )
    input_grad = grad_x_in.astype(jnp.bfloat16).reshape(docs, local_len, width)
    grad_columns = jnp.stack(
        [
            grad_bias_qkv[0:width],
            grad_bias_qkv[2 * width :],
            grad_bias_out,
            grad_bias_down,
            grad_gain1,
            grad_shift1,
            grad_gain2,
            grad_shift2,
        ],
        axis=1,
    )
    grad_smalls = jnp.concatenate(
        [
            grad_columns,
            jnp.transpose(grad_bias_up.reshape(FF // width, width)),
            jnp.transpose(grad_embed),
        ],
        axis=1,
    )
    qkv_shard, out_shard, up_shard, down_shard, small_shard = (
        lax.psum_scatter(
            grad_w_qkv.astype(jnp.bfloat16), "dp", scatter_dimension=0, tiled=True
        ).astype(jnp.float32),
        lax.psum_scatter(
            grad_w_out.astype(jnp.bfloat16), "dp", scatter_dimension=0, tiled=True
        ).astype(jnp.float32),
        lax.psum_scatter(
            grad_w_up.astype(jnp.bfloat16), "dp", scatter_dimension=0, tiled=True
        ).astype(jnp.float32),
        lax.psum_scatter(
            grad_w_down.astype(jnp.bfloat16), "dp", scatter_dimension=0, tiled=True
        ).astype(jnp.float32),
        lax.psum_scatter(
            grad_smalls.astype(jnp.bfloat16), "dp", scatter_dimension=0, tiled=True
        ).astype(jnp.float32),
    )
    mats_shard = jnp.concatenate([qkv_shard, out_shard, up_shard, down_shard], axis=1)
    mats_grad, smalls_grad = (
        lax.psum(mats_shard.astype(jnp.bfloat16), "seq").astype(jnp.float32),
        lax.psum(small_shard.astype(jnp.bfloat16), "seq").astype(jnp.float32),
    )
    out_bias_grad = smalls_grad[:, 2]
    total_tokens = rows * lax.axis_size("dp") * lax.axis_size("seq")
    rate = base_rate / math.sqrt(total_tokens)
    decayed = mats_grad + decay_rate * mats
    new_mats_momentum = momentum_rate * mats_momentum + decayed
    new_mats = mats - rate * (decayed + momentum_rate * new_mats_momentum)
    new_mats_average = average_rate * mats_average + (1.0 - average_rate) * new_mats
    new_smalls_momentum = momentum_rate * smalls_momentum + smalls_grad
    new_smalls = smalls - rate * (smalls_grad + momentum_rate * new_smalls_momentum)
    new_smalls_average = average_rate * smalls_average + (1.0 - average_rate) * new_smalls
    return (
        block_out,
        input_grad,
        mats_grad,
        new_mats,
        new_mats_momentum,
        new_mats_average,
        smalls_grad,
        out_bias_grad,
        new_smalls,
        new_smalls_momentum,
        new_smalls_average,
    )


def solution(mesh):
    placed = (
        P("dp", "seq", None),
        P("dp", None),
        P("dp", None),
        P("dp", "seq", None),
        P("dp", None),
        P("dp", None),
        P("dp", None),
        P("dp", None),
        P("dp", None),
        P("dp", None),
    )
    return jax.shard_map(
        per_device,
        mesh=mesh,
        in_specs=placed,
        out_specs=(
            P("dp", "seq", None),
            P("dp", "seq", None),
            P("dp", None),
            P("dp", None),
            P("dp", None),
            P("dp", None),
            P("dp", None),
            P("dp"),
            P("dp", None),
            P("dp", None),
            P("dp", None),
        ),
        check_vma=False,
    )
```

profile of v0, /device:TPU:0, one launch (start us, length us, event | category | flops | bytes accessed | tf_op | source)
XLA Modules:
  0.0 777.8 jit_solution(7473604885597649127)
XLA Ops:
  7.2 1.6 convert_element_type.179
  10.4 23.3 %all-gather.2 = bf16[16,48,15]{1,2,0:T(8,128)(2,1)S(1)} all-gather(bf16[1,48,15]{1,2,0:T(8,128)(2,1)S(1)} %convert_bitcast_fusion.1), channel_id=1, replica_groups=mesh['dp'=16,'seq'=2] {'dp'}, dimensions={0}, use_global_device_ids=true | all-gather | bytes 24480 | tf_op jit(solution)/shard_map/all_gather | solution.py:126
  34.9 25.7 %all-gather.10.cloned.1.call-done = bf16[768,2304]{1,0:T(8,128)(2,1)} async-done(((bf16[48,2304]{1,0:T(8,128)(2,1)}), bf16[768,2304]{1,0:T(8,128)(2,1)}) %all-gather.10.cloned.1.call-update) | async-done | bytes 3538960 | tf_op jit(solution)/shard_map/all_gather | solution.py:120
  60.6 4.0 fusion.13
  64.6 1.3 fusion.46
  69.5 22.8 %all-gather.20.cloned.1.call-done = bf16[1024,768]{1,0:T(8,128)(2,1)} async-done(((bf16[512,768]{1,0:T(8,128)(2,1)}), bf16[1024,768]{1,0:T(8,128)(2,1)}) %all-gather.20.cloned.1.call-update) | async-done | bytes 1572880 | tf_op jit(solution)/shard_map/all_gather | solution.py:146
  92.3 1.7 copy.37
  94.0 10.7 %fusion.6 = (f32[12,512]{1,0:T(8,128)S(1)}, f32[12,512,1024]{2,1,0:T(8,128)}) fusion(pred[1024]{0:T(1024)(128)(4,1)S(1)} %compare_reduce_fusion, bf16[512,12,64]{0,2,1:T(8,128)(2,1)S(1)} %bitcast.73, bf16[1024,12,64]{0,2,1:T(8,128)(2,1)S(1)} %bitcast.71), kind=kOutput, calls=%fused_computation.11 | convolution fusion | flops 824174592 | bytes 27550720 | tf_op jit(solution)/shard_map/while/body/eval_jaxpr/qhe,khe->hqk/dot_general | solution.py:48
  104.7 11.2 %fusion = f32[12,512]{1,0:T(8,128)S(1)} fusion(f32[12,512]{1,0:T(8,128)S(1)} %get-tuple-element.103, f32[12,512,1024]{2,1,0:T(8,128)} %get-tuple-element.104, pred[1024]{0:T(1024)(128)(4,1)S(1)} %compare_reduce_fusion), kind=kLoop, calls=%fused_computation.6 | loop fusion | flops 25159680 | bytes 25216000 | tf_op jit(solution)/shard_map/while/body/eval_jaxpr/reduce_sum | solution.py:62
  115.9 5.7 all-gather.18.cloned.1.call-done
  121.7 1.7 copy.35
  123.4 12.1 %fusion.21 = bf16[12,64,512]{2,1,0:T(8,128)(2,1)} fusion(bf16[1024,12,64]{0,2,1:T(8,128)(2,1)S(1)} %bitcast.76, f32[12,512]{1,0:T(8,128)S(1)} %fusion, f32[12,512]{1,0:T(8,128)S(1)} %get-tuple-element.103, f32[12,512,1024]{2,1,0:T(8,128)} %get-tuple-element.104, pred[1024]{0:T(1024)(128)(4,1)S(1)} %compare_reduce_fusion), kind=kOutput, calls=%fused_computation.65 | convolution fusion | flops 837156864 | bytes 27575296 | tf_op jit(solution)/shard_map/while/body/eval_jaxpr/hqk,khe->qhe/dot_general | solution.py:64
  135.5 27.3 %all-gather.12.cloned.1.call-done = bf16[768,768]{1,0:T(8,128)(2,1)} async-done(((bf16[48,768]{1,0:T(8,128)(2,1)}), bf16[768,768]{1,0:T(8,128)(2,1)}) %all-gather.12.cloned.1.call-update) | async-done | bytes 1179664 | tf_op jit(solution)/shard_map/all_gather | solution.py:121
  162.7 2.9 fusion.49
  166.0 51.8 %all-gather.14.cloned.1.call-done = bf16[768,3072]{1,0:T(8,128)(2,1)} async-done(((bf16[48,3072]{1,0:T(8,128)(2,1)}), bf16[768,3072]{1,0:T(8,128)(2,1)}) %all-gather.14.cloned.1.call-update) | async-done | bytes 4718608 | tf_op jit(solution)/shard_map/all_gather | solution.py:122
  217.8 19.8 %multiply_convert_fusion.1 = (bf16[512,3072]{1,0:T(8,128)(2,1)}, f32[512,3072]{1,0:T(8,128)}, f32[512,3072]{1,0:T(8,128)}) fusion(f32[3072]{0:T(1024)S(1)} %add.163, bf16[768,3072]{1,0:T(8,128)(2,1)} %all-gather.14.cloned.1.call-done, f32[512,768]{1,0:T(8,128)S(1)} %get-tuple-element.106, f32[768]{0:T(1024)S(1)} %get-tuple-element.70, ...), kind=kOutput, calls=%fused_computation.15 | convolution fusion | flops 2521694208 | bytes 22042624 | tf_op jit(solution)/shard_map/dot_general | solution.py:20
  237.6 34.9 %all-gather.16.cloned.1.call-done = bf16[768,3072]{1,0:T(8,128)(2,1)} async-done(((bf16[48,3072]{1,0:T(8,128)(2,1)}), bf16[768,3072]{1,0:T(8,128)(2,1)}) %all-gather.16.cloned.1.call-update) | async-done | bytes 4718608 | tf_op jit(solution)/shard_map/all_gather | solution.py:125
  272.5 6.6 fusion.50
  280.2 1.6 fusion.44
  282.0 1.9 copy-done.28
  283.9 7.0 fusion.40
  291.0 3.2 multiply_reduce_fusion.1
  294.8 1.1 copy-done.9
  297.1 1.7 convolution_convert_fusion.4
  298.8 1.4 copy.38
  300.2 12.6 %fusion.16 = bf16[12,64,1024]{2,1,0:T(8,128)(2,1)} fusion(bf16[512,12,64]{0,2,1:T(8,128)(2,1)S(1)} %bitcast.81, f32[12,512]{1,0:T(8,128)S(1)} %log_add_fusion, f32[12,512,1024]{2,1,0:T(8,128)} %get-tuple-element.104, pred[1024]{0:T(1024)(128)(4,1)S(1)} %compare_reduce_fusion), kind=kOutput, calls=%fused_computation.46 | convolution fusion | flops 831258624 | bytes 27550720 | tf_op jit(solution)/shard_map/while/body/eval_jaxpr/hqk,qhe->khe/dot_general | solution.py:83
  312.9 20.8 %multiply_reduce_fusion = (f32[12,512]{1,0:T(8,128)S(1)}, f32[12,512,1024]{2,1,0:T(8,128)}) fusion(f32[12,512]{1,0:T(8,128)S(1)} %log_add_fusion, f32[12,512,1024]{2,1,0:T(8,128)} %get-tuple-element.104, pred[1024]{0:T(1024)(128)(4,1)S(1)} %compare_reduce_fusion, bf16[512,12,64]{0,2,1:T(8,128)(2,1)S(1)} %bitcast.82, bf16[1024,12,64]{0,2,1:T(8,128)(2,1)S(1)} %bitcast.77), kind=kOutput, calls=%fused_computation.1 | convolution fusion | flops 836757504 | bytes 52741120 | tf_op jit(solution)/shard_map/while/body/eval_jaxpr/qhe,khe->hqk/dot_general | solution.py:80
  333.7 16.9 %multiply_convert_fusion = bf16[12,512,1024]{2,1,0:T(8,128)(2,1)S(1)} fusion(f32[12,512,1024]{2,1,0:T(8,128)} %get-tuple-element.112, f32[12,512]{1,0:T(8,128)S(1)} %get-tuple-element.111, f32[12,512]{1,0:T(8,128)S(1)} %log_add_fusion, f32[12,512,1024]{2,1,0:T(8,128)} %get-tuple-element.104, pred[1024]{0:T(1024)(128)(4,1)S(1)} %compare_reduce_fusion), kind=kLoop, calls=%fused_computation | loop fusion | flops 37748736 | bytes 62964736 | tf_op jit(solution)/shard_map/while/body/eval_jaxpr/convert_element_type | solution.py:87
  350.6 4.1 multiply_convert_fusion.2
  354.7 1.0 copy-done.2
  355.8 3.0 convolution_convert_fusion.3
  358.9 6.8 convolution_convert_fusion.1
  365.8 1.1 copy-done.18
  366.9 6.3 convolution_convert_fusion
  373.4 1.2 copy-done.4
  374.5 8.6 %multiply_convert_fusion.3 = bf16[12,64,512]{2,1,0:T(8,128)(2,1)S(1)} fusion(bf16[1024,12,64]{0,2,1:T(8,128)(2,1)S(1)} %bitcast.72, bf16[12,512,1024]{2,1,0:T(8,128)(2,1)} %copy-done.2), kind=kOutput, calls=%fused_computation.51 | convolution fusion | flops 806092800 | bytes 14942208 | tf_op jit(solution)/shard_map/while/body/eval_jaxpr/hqk,khe->qhe/dot_general | solution.py:89
  383.2 5.9 convolution_convert_fusion.2
  389.4 1.9 fusion.36
  391.4 4.9 add_add_fusion.4
  398.1 44.1 %reduce-scatter.16.cloned.1.call-done = bf16[48,768]{1,0:T(8,128)(2,1)} async-done(((bf16[768,768]{1,0:T(8,128)(2,1)}), bf16[48,768]{1,0:T(8,128)(2,1)}) %reduce-scatter.16.cloned.1.call-update) | async-done | bytes 73744 | tf_op jit(solution)/shard_map/reduce_scatter | solution.py:253
  442.3 78.3 %reduce-scatter.18.cloned.1.call-done = bf16[48,3072]{1,0:T(8,128)(2,1)} async-done(((bf16[768,3072]{1,0:T(8,128)(2,1)}), bf16[48,3072]{1,0:T(8,128)(2,1)}) %reduce-scatter.18.cloned.1.call-update) | async-done | bytes 294928 | tf_op jit(solution)/shard_map/reduce_scatter | solution.py:256
  520.5 79.0 %reduce-scatter.20.cloned.1.call-done = bf16[48,3072]{1,0:T(8,128)(2,1)} async-done(((bf16[768,3072]{1,0:T(8,128)(2,1)}), bf16[48,3072]{1,0:T(8,128)(2,1)}) %reduce-scatter.20.cloned.1.call-update) | async-done | bytes 294928 | tf_op jit(solution)/shard_map/reduce_scatter | solution.py:259
  599.5 70.9 %reduce-scatter.14.cloned.1.call-done = bf16[48,2304]{1,0:T(8,128)(2,1)} async-done(((bf16[768,2304]{1,0:T(8,128)(2,1)}), bf16[48,2304]{1,0:T(8,128)(2,1)}) %reduce-scatter.14.cloned.1.call-update) | async-done | bytes 221200 | tf_op jit(solution)/shard_map/reduce_scatter | solution.py:250
  670.4 2.1 pad_maximum_fusion.1
  673.5 53.5 %reduce-scatter.22.cloned.1.call-done = bf16[48,15]{1,0:T(8,128)(2,1)} async-done(((bf16[768,15]{1,0:T(8,128)(2,1)}), bf16[48,15]{1,0:T(8,128)(2,1)}) %reduce-scatter.22.cloned.1.call-update) | async-done | bytes 1456
  727.8 4.9 psum.15
  733.9 31.4 %all-reduce.2.cloned.1.call-done = bf16[48,9216]{1,0:T(8,128)(2,1)} async-done(((bf16[48,9216]{1,0:T(8,128)(2,1)}), bf16[48,9216]{1,0:T(8,128)(2,1)}) %all-reduce.2.cloned.1.call-update) | async-done | bytes 884752 | tf_op jit(solution)/shard_map/psum | solution.py:268
  765.3 5.7 multiply_add_fusion
  (143 shorter events, 15.0 us)
Async XLA Ops:
  7.2 26.7 %copy-start = (s32[1,1024]{1,0:T(1,128)S(1)}, s32[1,1024]{1,0:T(1,128)}, u32[]{:S(2)}) copy-start(s32[1,1024]{1,0:T(1,128)} %param.11) | copy-start | bytes 12292
  7.2 27.3 %copy-start.16 = (bf16[1,512,768]{2,1,0:T(8,128)(2,1)S(1)}, bf16[1,512,768]{2,1,0:T(8,128)(2,1)}, u32[]{:S(2)}) copy-start(bf16[1,512,768]{2,1,0:T(8,128)(2,1)} %param.10) | copy-start | bytes 2359300
  7.2 53.4 %all-gather.10.cloned.1.call-start = ((), (), s32[]{:S(2)}) async-start(), calls=%async_computation.7 | async-start | bytes 3760128 | tf_op jit(solution)/shard_map/all_gather | solution.py:120
  9.6 82.7 %all-gather.20.cloned.1.call-start = ((), (), s32[]{:S(2)}) async-start(), calls=%async_computation.19 | async-start | bytes 2359296 | tf_op jit(solution)/shard_map/all_gather | solution.py:146
  33.9 0.6 copy-start.22
  34.9 25.7 %copy-start.15 = (f32[512,768]{1,0:T(8,128)}, f32[512,768]{1,0:T(8,128)S(1)}, u32[]{:S(2)}) copy-start(f32[512,768]{1,0:T(8,128)S(1)} %convert_add_fusion) | copy-start | bytes 4718596
  64.6 4.5 copy-start.27
  65.9 55.7 %all-gather.18.cloned.1.call-start = ((), (), s32[]{:S(2)}) async-start(), calls=%async_computation.18 | async-start | bytes 2359296 | tf_op jit(solution)/shard_map/all_gather | solution.py:147
  66.7 96.1 %all-gather.12.cloned.1.call-start = ((), (), s32[]{:S(2)}) async-start(), calls=%async_computation.8 | async-start | bytes 1253376 | tf_op jit(solution)/shard_map/all_gather | solution.py:121
  67.4 150.4 %all-gather.14.cloned.1.call-start = ((), (), s32[]{:S(2)}) async-start(), calls=%async_computation.9 | async-start | bytes 5013504 | tf_op jit(solution)/shard_map/all_gather | solution.py:122
  68.3 204.2 %all-gather.16.cloned.1.call-start = ((), (), s32[]{:S(2)}) async-start(), calls=%async_computation.10 | async-start | bytes 5013504 | tf_op jit(solution)/shard_map/all_gather | solution.py:125
  68.9 314.3 %reduce-scatter.12.cloned.1.call-start = ((), (), s32[]{:S(2)}) async-start(), calls=%async_computation.12 | async-start | bytes 2359296 | tf_op jit(solution)/shard_map/reduce_scatter | solution.py:205
  69.4 35.2 %copy-start.5 = (bf16[512,768]{0,1:T(8,128)(2,1)}, bf16[512,768]{0,1:T(8,128)(2,1)S(1)}, u32[]{:S(2)}) copy-start(bf16[512,768]{0,1:T(8,128)(2,1)S(1)} %copy.36) | copy-start | bytes 2359300
  94.0 10.7 %copy-start.3 = (bf16[1024,768]{0,1:T(8,128)(2,1)}, bf16[1024,768]{0,1:T(8,128)(2,1)S(1)}, u32[]{:S(2)}) copy-start(bf16[1024,768]{0,1:T(8,128)(2,1)S(1)} %copy.37) | copy-start | bytes 4718596
  165.7 72.0 %copy-start.11 = (f32[512,768]{1,0:T(8,128)}, f32[512,768]{1,0:T(8,128)S(1)}, u32[]{:S(2)}) copy-start(f32[512,768]{1,0:T(8,128)S(1)} %get-tuple-element.106) | copy-start | bytes 4718596
  272.5 6.9 copy-start.8
  279.1 2.9 copy-start.31
  279.4 4.5 copy-start.28
  280.2 10.8 %slice-start = ((s8[4718592]{0:T(1024)(128)(4,1)}), s8[4194304]{0:T(1024)(128)(4,1)S(1)}, s32[]{:S(2)}) async-start(s8[4718592]{0:T(1024)(128)(4,1)} %bitcast.93), calls=%async_computation.21 | async-start | bytes 8388608
  282.0 8.9 %copy-start.17 = (bf16[512,768]{1,0:T(8,128)(2,1)}, bf16[512,768]{1,0:T(8,128)(2,1)S(1)}, u32[]{:S(2)}) copy-start(bf16[512,768]{1,0:T(8,128)(2,1)S(1)} %get-tuple-element.82) | copy-start | bytes 2359300
  283.9 7.1 copy-start.12
  283.9 7.1 slice-start.1
  290.9 3.2 copy-start.30
  294.2 2.9 copy-start.29
  294.8 1.1 copy-start.9
  296.2 0.9 copy-start.19
  312.9 70.3 %reduce-scatter.10.cloned.1.call-start = ((), (), s32[]{:S(2)}) async-start(), calls=%async_computation.11 | async-start | bytes 2359296 | tf_op jit(solution)/shard_map/reduce_scatter | solution.py:202
  333.7 16.9 %copy-start.6 = (bf16[512,768]{0,1:T(8,128)(2,1)S(1)}, bf16[512,768]{0,1:T(8,128)(2,1)}, u32[]{:S(2)}) copy-start(bf16[512,768]{0,1:T(8,128)(2,1)} %copy-done.5) | copy-start | bytes 2359300
  350.6 5.1 copy-start.2
  350.6 5.2 copy-start.20
  355.7 3.2 copy-start.13
  355.7 86.6 %reduce-scatter.16.cloned.1.call-start = ((), (), s32[]{:S(2)}) async-start(), calls=%async_computation.14 | async-start | bytes 1253376 | tf_op jit(solution)/shard_map/reduce_scatter | solution.py:253
  358.8 161.7 %reduce-scatter.18.cloned.1.call-start = ((), (), s32[]{:S(2)}) async-start(), calls=%async_computation.15 | async-start | bytes 5013504 | tf_op jit(solution)/shard_map/reduce_scatter | solution.py:256
  365.7 1.1 copy-start.18
  365.8 233.8 %reduce-scatter.20.cloned.1.call-start = ((), (), s32[]{:S(2)}) async-start(), calls=%async_computation.16 | async-start | bytes 5013504 | tf_op jit(solution)/shard_map/reduce_scatter | solution.py:259
  373.1 1.4 copy-start.4
  373.2 297.3 %reduce-scatter.14.cloned.1.call-start = ((), (), s32[]{:S(2)}) async-start(), calls=%async_computation.13 | async-start | bytes 3760128 | tf_op jit(solution)/shard_map/reduce_scatter | solution.py:250
  383.1 6.3 copy-start.14
  389.1 2.3 copy-start.10
  389.1 337.9 %reduce-scatter.22.cloned.1.call-start = ((), (), s32[]{:S(2)}) async-start(), calls=%async_computation.20 | async-start | bytes 208896
  391.4 5.0 copy-start.23
  396.4 336.4 %copy-start.21 = (f32[48,15]{0,1:T(8,128)S(1)}, f32[48,15]{0,1:T(8,128)}, u32[]{:S(2)}) copy-start(f32[48,15]{0,1:T(8,128)} %param.17) | copy-start | bytes 8644
  396.4 336.4 %copy-start.24 = (f32[48,15]{0,1:T(8,128)S(1)}, f32[48,15]{0,1:T(8,128)}, u32[]{:S(2)}) copy-start(f32[48,15]{0,1:T(8,128)} %param.19) | copy-start | bytes 8644
  396.4 336.4 %copy-start.25 = (f32[48,15]{0,1:T(8,128)S(1)}, f32[48,15]{0,1:T(8,128)}, u32[]{:S(2)}) copy-start(f32[48,15]{0,1:T(8,128)} %param.18) | copy-start | bytes 8644
  396.4 368.9 %copy-start.7 = (f32[48,9216]{1,0:T(8,128)S(1)}, f32[48,9216]{1,0:T(8,128)}, u32[]{:S(2)}) copy-start(f32[48,9216]{1,0:T(8,128)} %param.14) | copy-start | bytes 5308420
  398.1 367.2 %all-reduce.2.cloned.1.call-start = ((), (), s32[]{:S(2)}) async-start(), calls=%async_computation.17 | async-start | bytes 1769472 | tf_op jit(solution)/shard_map/psum | solution.py:268
  733.4 37.7 %copy-start.26 = (f32[48,15]{0,1:T(8,128)}, f32[48,15]{0,1:T(8,128)S(1)}, u32[]{:S(2)}) copy-start(f32[48,15]{0,1:T(8,128)S(1)} %get-tuple-element.78) | copy-start | bytes 8644
  733.4 37.7 %copy-start.1 = (s32[1,1024]{1,0:T(1,128)S(1)}, s32[1,1024]{1,0:T(1,128)}, u32[]{:S(2)}) copy-start(s32[1,1024]{1,0:T(1,128)} %param.11) | copy-start | bytes 12292
Sparse Core Ops, SparseCore 0:
  10.9 49.6 all-gather.9
  66.0 26.1 all-gather.19
  94.4 27.2 all-gather.17
  124.4 38.3 all-gather.11
  165.4 52.3 all-gather.13
  220.5 51.9 all-gather.15
  313.0 24.5 reduce-scatter.11
  355.8 24.6 reduce-scatter.9
  384.1 58.1 reduce-scatter.15
  446.0 74.5 reduce-scatter.17
  524.9 74.5 reduce-scatter.19
  603.3 67.1 reduce-scatter.13
  674.5 52.4 reduce-scatter.21
  729.8 35.4 all-reduce.1
where the time goes:
time: 781 us; the launch traced here: 778 us
  waiting for transfers between devices  527 us (67%)
  matrix products  142 us (18%)
  other arithmetic  46.1 us (6%)
  blocking collectives  28.3 us (4%)
  local copies, waits for them, and re-layouts  18.8 us (2%)
  between operations  14.7 us (2%)
    reduce_scatter x1, waiting for transfers between devices, per_device(): lax.psum_scatter(grad_w_down.astype(jnp.bfloat16), 'dp', scatter_dimensio...  79 us
    reduce_scatter x1, waiting for transfers between devices, per_device(): lax.psum_scatter(grad_w_up.astype(jnp.bfloat16), 'dp', scatter_dimension=...  78.3 us
    reduce_scatter x1, waiting for transfers between devices, per_device(): lax.psum_scatter(grad_w_qkv.astype(jnp.bfloat16), 'dp', scatter_dimension...  70.9 us
    unnamed x15, waiting for transfers between devices  54.9 us
    all_gather x1, waiting for transfers between devices, per_device(): lax.all_gather(low_mats[:, 4 * MODEL_WIDTH:4 * MODEL_WIDTH + FF], 'dp', a...  51.8 us
    reduce_scatter x1, waiting for transfers between devices, per_device(): lax.psum_scatter(grad_w_out.astype(jnp.bfloat16), 'dp', scatter_dimension...  44.1 us
    all_gather x1, waiting for transfers between devices, per_device(): lax.all_gather(low_mats[:, 4 * MODEL_WIDTH + FF:], 'dp', axis=0, tiled=True)  34.9 us
    dot_general x5, matrix products, product(): return jnp.dot(left, right, preferred_element_type=jnp.float32)  34.2 us
  transfers between devices with their start and end apart: 14, of which 12 were waited for; matrix products, arithmetic and copies ran while one was open for 19% of the time, Pallas kernels for 0%

commit v1 on v0

--- a/solution.py
+++ b/solution.py
@@ -14,6 +14,25 @@
 average_rate = 0.75
 base_rate = 0.03
 masked_score = -1e30
+
+
+def _post_desk(u, along_axis):
+    small, tall, formed = (
+        jax.lax.axis_size(along_axis),
+        jax.lax.axis_index(along_axis),
+        u.shape[0],
+    )
+    local_now, seen_now = (u, 1)
+    while seen_now < small:
+        pieces_in = []
+        for pp in range(small):
+            pieces_in.append((pp, (pp - seen_now) % small))
+        local_now = jnp.concatenate(
+            [local_now, jax.lax.ppermute(local_now, axis_name=along_axis, perm=pieces_in)], axis=0
+        )
+        seen_now = 2 * seen_now
+    local_out = jnp.roll(local_now, shift=tall * formed, axis=0)
+    return local_out
 
 
 def product(left, right):
@@ -119,9 +138,7 @@
     w_qkv, w_out, w_up, w_down, whole_smalls = (
         lax.all_gather(low_mats[:, 0 : 3 * MODEL_WIDTH], "dp", axis=0, tiled=True),
         lax.all_gather(low_mats[:, 3 * MODEL_WIDTH : 4 * MODEL_WIDTH], "dp", axis=0, tiled=True),
-        lax.all_gather(
-            low_mats[:, 4 * MODEL_WIDTH : 4 * MODEL_WIDTH + FF], "dp", axis=0, tiled=True
-        ),
+        _post_desk(low_mats[:, 4 * MODEL_WIDTH : 4 * MODEL_WIDTH + FF], "dp"),
         lax.all_gather(low_mats[:, 4 * MODEL_WIDTH + FF :], "dp", axis=0, tiled=True),
         lax.all_gather(smalls.astype(jnp.bfloat16), "dp", axis=0, tiled=True),
     )

time: 781 us -> 825 us (1.056)
  local copies, waits for them, and re-layouts: 18.8 us -> 33.8 us
  waiting for transfers between devices: 527 us -> 539 us
  starting transfers between devices: 0.92 us -> 11.5 us
    ppermute x0 -> x4, waiting for transfers between devices: none -> 133 us  [_post_desk(): jax.lax.ppermute(local_now, axis_name=along_axis, perm=pieces_in)]
    all_gather x1, waiting for transfers between devices: 34.9 us -> 0.02 us  [per_device(): lax.all_gather(low_mats[:, 4 * MODEL_WIDTH + FF:], 'dp', axis=0, tiled=True)]
    all_gather x1, waiting for transfers between devices: 51.8 us -> 18.7 us  [per_device(): lax.all_gather(low_mats[:, 4 * MODEL_WIDTH:4 * MODEL_WIDTH + FF], 'dp', a...]
    all_gather x1, waiting for transfers between devices: 27.3 us -> 0.01 us  [per_device(): lax.all_gather(low_mats[:, 3 * MODEL_WIDTH:4 * MODEL_WIDTH], 'dp', axis=0...]
    all_gather x1, waiting for transfers between devices: 22.8 us -> 0.02 us  [per_device(): lax.all_gather(keys_local, 'seq', axis=1, tiled=True)]
    ppermute x0 -> x4, starting transfers between devices: none -> 10.6 us  [_post_desk(): jax.lax.ppermute(local_now, axis_name=along_axis, perm=pieces_in)]
    unnamed x71 -> x88, local copies, waits for them, and re-layouts: 9.46 us -> 19.4 us
  transfers between devices with their start and end apart: 14 -> 18, of which waited for: 12 -> 10; matrix products, arithmetic and copies ran while one was open for 19% -> 23% of each run, Pallas kernels for 0% -> 0%
where the time goes in v1:
time: 825 us; the launch traced here: 821 us
  waiting for transfers between devices  539 us (65%)
  matrix products  148 us (18%)
  other arithmetic  48.3 us (6%)
  local copies, waits for them, and re-layouts  33.8 us (4%)
  blocking collectives  25 us (3%)
  between operations  14.8 us (2%)
  starting transfers between devices  11.5 us (1%)
    ppermute x4, waiting for transfers between devices, _post_desk(): jax.lax.ppermute(local_now, axis_name=along_axis, perm=pieces_in)  133 us
    reduce_scatter x1, waiting for transfers between devices, per_device(): lax.psum_scatter(grad_w_down.astype(jnp.bfloat16), 'dp', scatter_dimensio...  78.9 us
    reduce_scatter x1, waiting for transfers between devices, per_device(): lax.psum_scatter(grad_w_up.astype(jnp.bfloat16), 'dp', scatter_dimension=...  78.3 us
    reduce_scatter x1, waiting for transfers between devices, per_device(): lax.psum_scatter(grad_w_qkv.astype(jnp.bfloat16), 'dp', scatter_dimension...  70.9 us
    unnamed x15, waiting for transfers between devices  54.2 us
    reduce_scatter x1, waiting for transfers between devices, per_device(): lax.psum_scatter(grad_w_out.astype(jnp.bfloat16), 'dp', scatter_dimension...  44.1 us
    dot_general x5, matrix products, product(): return jnp.dot(left, right, preferred_element_type=jnp.float32)  36 us
    psum x1, waiting for transfers between devices, per_device(): lax.psum(mats_shard.astype(jnp.bfloat16), 'seq').astype(jnp.float32)  31.4 us
  transfers between devices with their start and end apart: 18, of which 10 were waited for; matrix products, arithmetic and copies ran while one was open for 23% of the time, Pallas kernels for 0%

profile of v1, /device:TPU:0, one launch (start us, length us, event | category | flops | bytes accessed | tf_op | source)
XLA Modules:
  0.0 820.9 jit_solution(6704853497668655015)
XLA Ops:
  7.3 1.6 convert_element_type.179
  10.5 5.4 collective-permute-start
  15.9 20.1 %all-gather.2 = bf16[16,48,15]{1,2,0:T(8,128)(2,1)S(1)} all-gather(bf16[1,48,15]{1,2,0:T(8,128)(2,1)S(1)} %convert_bitcast_fusion.1), channel_id=1, replica_groups=mesh['dp'=16,'seq'=2] {'dp'}, dimensions={0}, use_global_device_ids=true | all-gather | bytes 24480 | tf_op jit(solution)/shard_map/all_gather | solution.py:143
  36.9 1.6 convert_add_fusion
  38.6 30.2 %all-gather.10.cloned.1.call-done = bf16[768,2304]{1,0:T(8,128)(2,1)} async-done(((bf16[48,2304]{1,0:T(8,128)(2,1)}), bf16[768,2304]{1,0:T(8,128)(2,1)}) %all-gather.10.cloned.1.call-update) | async-done | bytes 3538960 | tf_op jit(solution)/shard_map/all_gather | solution.py:139
  68.8 4.5 fusion.15
  73.3 1.4 fusion.48
  75.9 3.7 collective-permute-start.2
  79.7 25.9 %collective-permute-done.2 = bf16[192,3072]{1,0:T(8,128)(2,1)S(1)} collective-permute-done((bf16[192,3072]{1,0:T(8,128)(2,1)}, bf16[192,3072]{1,0:T(8,128)(2,1)S(1)}, u32[]{:S(2)}, u32[]{:S(2)}) %collective-permute-start.2) | collective-permute-done | bytes 1179680 | tf_op jit(solution)/shard_map/ppermute | solution.py:31
  105.6 1.5 pad_maximum_fusion
  107.1 1.4 collective-permute-start.3
  112.0 106.7 %collective-permute-done.3 = bf16[384,3072]{1,0:T(8,128)(2,1)} collective-permute-done((bf16[384,3072]{1,0:T(8,128)(2,1)}, bf16[384,3072]{1,0:T(8,128)(2,1)}, u32[]{:S(2)}, u32[]{:S(2)}) %collective-permute-start.3) | collective-permute-done | bytes 2359328 | tf_op jit(solution)/shard_map/ppermute | solution.py:31
  218.7 3.3 constant_dynamic-update-slice_fusion.5
  226.5 3.2 constant_dynamic-update-slice_fusion
  230.0 2.0 copy.37
  232.0 10.2 %fusion.6 = (f32[12,512]{1,0:T(8,128)S(1)}, f32[12,512,1024]{2,1,0:T(8,128)}) fusion(pred[1024]{0:T(1024)(128)(4,1)S(1)} %compare_reduce_fusion, bf16[512,12,64]{0,2,1:T(8,128)(2,1)S(1)} %bitcast.72, bf16[1024,12,64]{0,2,1:T(8,128)(2,1)S(1)} %bitcast.70), kind=kOutput, calls=%fused_computation.11 | convolution fusion | flops 824174592 | bytes 27550720 | tf_op jit(solution)/shard_map/while/body/eval_jaxpr/qhe,khe->hqk/dot_general | solution.py:67
  242.2 11.5 %fusion = f32[12,512]{1,0:T(8,128)S(1)} fusion(f32[12,512]{1,0:T(8,128)S(1)} %get-tuple-element.105, f32[12,512,1024]{2,1,0:T(8,128)} %get-tuple-element.106, pred[1024]{0:T(1024)(128)(4,1)S(1)} %compare_reduce_fusion), kind=kLoop, calls=%fused_computation.6 | loop fusion | flops 25159680 | bytes 25216000 | tf_op jit(solution)/shard_map/while/body/eval_jaxpr/reduce_sum | solution.py:81
  253.8 1.7 copy.35
  255.5 12.3 %fusion.23 = bf16[12,64,512]{2,1,0:T(8,128)(2,1)} fusion(bf16[1024,12,64]{0,2,1:T(8,128)(2,1)S(1)} %bitcast.75, f32[12,512]{1,0:T(8,128)S(1)} %fusion, f32[12,512]{1,0:T(8,128)S(1)} %get-tuple-element.105, f32[12,512,1024]{2,1,0:T(8,128)} %get-tuple-element.106, pred[1024]{0:T(1024)(128)(4,1)S(1)} %compare_reduce_fusion), kind=kOutput, calls=%fused_computation.68 | convolution fusion | flops 837156864 | bytes 27575296 | tf_op jit(solution)/shard_map/while/body/eval_jaxpr/hqk,khe->qhe/dot_general | solution.py:83
  267.8 2.4 fusion.52
  271.4 21.4 %multiply_convert_fusion.1 = (bf16[512,3072]{1,0:T(8,128)(2,1)}, f32[512,3072]{1,0:T(8,128)}, f32[512,3072]{1,0:T(8,128)}) fusion(f32[3072]{0:T(1024)S(1)} %add.175, bf16[1536,3072]{1,0:T(8,128)(2,1)} %constant_dynamic-update-slice_fusion, s32[]{:T(128)S(6)} %select_n.26, f32[512,768]{1,0:T(8,128)S(1)} %get-tuple-element.108, f32[768]{0:T(1024)S(1)} %copy-done.31, ...), kind=kOutput, calls=%fused_computation.15 | convolution fusion | flops 2521694208 | bytes 22042628 | tf_op jit(solution)/shard_map/dot_general | solution.py:39
  292.9 6.7 fusion.53
  300.7 1.6 fusion.46
  305.3 6.1 fusion.42
  311.5 18.7 %all-gather.16.cloned.1.call-done = bf16[768,3072]{1,0:T(8,128)(2,1)} async-done(((bf16[48,3072]{1,0:T(8,128)(2,1)}), bf16[768,3072]{1,0:T(8,128)(2,1)}) %all-gather.16.cloned.1.call-update) | async-done | bytes 4718608 | tf_op jit(solution)/shard_map/all_gather | solution.py:183
  330.1 7.4 multiply_reduce_fusion.1
  340.4 1.7 convolution_convert_fusion.4
  342.1 1.4 copy.38
  343.5 12.6 %fusion.18 = bf16[12,64,1024]{2,1,0:T(8,128)(2,1)} fusion(bf16[512,12,64]{0,2,1:T(8,128)(2,1)S(1)} %bitcast.80, f32[12,512]{1,0:T(8,128)S(1)} %log_add_fusion, f32[12,512,1024]{2,1,0:T(8,128)} %get-tuple-element.106, pred[1024]{0:T(1024)(128)(4,1)S(1)} %compare_reduce_fusion), kind=kOutput, calls=%fused_computation.49 | convolution fusion | flops 831258624 | bytes 27550720 | tf_op jit(solution)/shard_map/while/body/eval_jaxpr/hqk,qhe->khe/dot_general | solution.py:102
  356.2 20.8 %multiply_reduce_fusion = (f32[12,512]{1,0:T(8,128)S(1)}, f32[12,512,1024]{2,1,0:T(8,128)}) fusion(f32[12,512]{1,0:T(8,128)S(1)} %log_add_fusion, f32[12,512,1024]{2,1,0:T(8,128)} %get-tuple-element.106, pred[1024]{0:T(1024)(128)(4,1)S(1)} %compare_reduce_fusion, bf16[512,12,64]{0,2,1:T(8,128)(2,1)S(1)} %bitcast.81, bf16[1024,12,64]{0,2,1:T(8,128)(2,1)S(1)} %bitcast.76), kind=kOutput, calls=%fused_computation.1 | convolution fusion | flops 836757504 | bytes 52741120 | tf_op jit(solution)/shard_map/while/body/eval_jaxpr/qhe,khe->hqk/dot_general | solution.py:99
  377.0 16.9 %multiply_convert_fusion = bf16[12,512,1024]{2,1,0:T(8,128)(2,1)S(1)} fusion(f32[12,512,1024]{2,1,0:T(8,128)} %get-tuple-element.114, f32[12,512]{1,0:T(8,128)S(1)} %get-tuple-element.113, f32[12,512]{1,0:T(8,128)S(1)} %log_add_fusion, f32[12,512,1024]{2,1,0:T(8,128)} %get-tuple-element.106, pred[1024]{0:T(1024)(128)(4,1)S(1)} %compare_reduce_fusion), kind=kLoop, calls=%fused_computation | loop fusion | flops 37748736 | bytes 62964736 | tf_op jit(solution)/shard_map/while/body/eval_jaxpr/convert_element_type | solution.py:106
  394.0 4.1 multiply_convert_fusion.2
  399.1 3.1 convolution_convert_fusion.3
  402.2 6.9 convolution_convert_fusion.1
  410.2 6.3 convolution_convert_fusion
  417.9 8.6 %multiply_convert_fusion.3 = bf16[12,64,512]{2,1,0:T(8,128)(2,1)S(1)} fusion(bf16[1024,12,64]{0,2,1:T(8,128)(2,1)S(1)} %bitcast.71, bf16[12,512,1024]{2,1,0:T(8,128)(2,1)} %copy-done.2), kind=kOutput, calls=%fused_computation.54 | convolution fusion | flops 806092800 | bytes 14942208 | tf_op jit(solution)/shard_map/while/body/eval_jaxpr/hqk,khe->qhe/dot_general | solution.py:108
  426.6 5.9 convolution_convert_fusion.2
  432.8 1.9 fusion.39
  434.8 4.9 add_add_fusion.4
  441.5 44.1 %reduce-scatter.16.cloned.1.call-done = bf16[48,768]{1,0:T(8,128)(2,1)} async-done(((bf16[768,768]{1,0:T(8,128)(2,1)}), bf16[48,768]{1,0:T(8,128)(2,1)}) %reduce-scatter.16.cloned.1.call-update) | async-done | bytes 73744 | tf_op jit(solution)/shard_map/reduce_scatter | solution.py:270
  485.6 78.3 %reduce-scatter.18.cloned.1.call-done = bf16[48,3072]{1,0:T(8,128)(2,1)} async-done(((bf16[768,3072]{1,0:T(8,128)(2,1)}), bf16[48,3072]{1,0:T(8,128)(2,1)}) %reduce-scatter.18.cloned.1.call-update) | async-done | bytes 294928 | tf_op jit(solution)/shard_map/reduce_scatter | solution.py:273
  563.9 78.9 %reduce-scatter.20.cloned.1.call-done = bf16[48,3072]{1,0:T(8,128)(2,1)} async-done(((bf16[768,3072]{1,0:T(8,128)(2,1)}), bf16[48,3072]{1,0:T(8,128)(2,1)}) %reduce-scatter.20.cloned.1.call-update) | async-done | bytes 294928 | tf_op jit(solution)/shard_map/reduce_scatter | solution.py:276
  642.8 70.9 %reduce-scatter.14.cloned.1.call-done = bf16[48,2304]{1,0:T(8,128)(2,1)} async-done(((bf16[768,2304]{1,0:T(8,128)(2,1)}), bf16[48,2304]{1,0:T(8,128)(2,1)}) %reduce-scatter.14.cloned.1.call-update) | async-done | bytes 221200 | tf_op jit(solution)/shard_map/reduce_scatter | solution.py:267
  713.6 2.1 pad_maximum_fusion.3
  716.7 53.4 %reduce-scatter.22.cloned.1.call-done = bf16[48,15]{1,0:T(8,128)(2,1)} async-done(((bf16[768,15]{1,0:T(8,128)(2,1)}), bf16[48,15]{1,0:T(8,128)(2,1)}) %reduce-scatter.22.cloned.1.call-update) | async-done | bytes 1456
  770.9 4.9 psum.15
  777.0 31.4 %all-reduce.2.cloned.1.call-done = bf16[48,9216]{1,0:T(8,128)(2,1)} async-done(((bf16[48,9216]{1,0:T(8,128)(2,1)}), bf16[48,9216]{1,0:T(8,128)(2,1)}) %all-reduce.2.cloned.1.call-update) | async-done | bytes 884752 | tf_op jit(solution)/shard_map/psum | solution.py:285
  808.4 5.7 multiply_add_fusion
  (172 shorter events, 28.7 us)
Async XLA Ops:
  7.2 29.7 %copy-start = (s32[1,1024]{1,0:T(1,128)S(1)}, s32[1,1024]{1,0:T(1,128)}, u32[]{:S(2)}) copy-start(s32[1,1024]{1,0:T(1,128)} %param.11) | copy-start | bytes 12292
  7.2 8.7 %copy-start.24 = (f32[48,15]{0,1:T(8,128)S(1)}, f32[48,15]{0,1:T(8,128)}, u32[]{:S(2)}) copy-start(f32[48,15]{0,1:T(8,128)} %param.17) | copy-start | bytes 8644
  7.2 29.7 %copy-start.19 = (bf16[1,512,768]{2,1,0:T(8,128)(2,1)S(1)}, bf16[1,512,768]{2,1,0:T(8,128)(2,1)}, u32[]{:S(2)}) copy-start(bf16[1,512,768]{2,1,0:T(8,128)(2,1)} %param.10) | copy-start | bytes 2359300
  7.2 61.6 %all-gather.10.cloned.1.call-start = ((), (), s32[]{:S(2)}) async-start(), calls=%async_computation.7 | async-start | bytes 3760128 | tf_op jit(solution)/shard_map/all_gather | solution.py:139
  9.6 220.4 %all-gather.20.cloned.1.call-start = ((), (), s32[]{:S(2)}) async-start(), calls=%async_computation.19 | async-start | bytes 2359296 | tf_op jit(solution)/shard_map/all_gather | solution.py:163
  10.5 95.1 %copy-start.7 = (bf16[48,3072]{1,0:T(8,128)(2,1)}, bf16[48,3072]{1,0:T(8,128)(2,1)S(1)}, u32[]{:S(2)}) copy-start(bf16[48,3072]{1,0:T(8,128)(2,1)S(1)} %get-tuple-element.101) | copy-start | bytes 884740
  10.5 28.0 %collective-permute-start = (bf16[48,3072]{1,0:T(8,128)(2,1)S(1)}, bf16[48,3072]{1,0:T(8,128)(2,1)S(1)}, u32[]{:S(2)}, u32[]{:S(2)}) collective-permute-start(bf16[48,3072]{1,0:T(8,128)(2,1)S(1)} %get-tuple-element.101), channel_id=1, source_target_pairs={{0,30},{2,0},{4,2},{6,4},{8,6},{10,8},{12,10},{14,12},{16,14},{18,... | collective-permute-start | bytes 884744 | tf_op jit(solution)/shard_map/ppermute | solution.py:31
  36.9 36.4 %copy-start.26 = (s32[1,512]{1,0:T(1,128)}, s32[1,512]{1,0:T(1,128)S(1)}, u32[]{:S(2)}) copy-start(s32[1,512]{1,0:T(1,128)S(1)} %constant_dynamic-slice_fusion) | copy-start | bytes 6148
  38.5 36.3 %collective-permute-start.1 = (bf16[96,3072]{1,0:T(8,128)(2,1)S(1)}, bf16[96,3072]{1,0:T(8,128)(2,1)S(1)}, u32[]{:S(2)}, u32[]{:S(2)}) collective-permute-start(bf16[96,3072]{1,0:T(8,128)(2,1)S(1)} %pad_maximum_fusion.4), channel_id=1, source_target_pairs={{0,28},{2,30},{4,0},{6,2},{8,4},{10,6},{12,8},{14,10},{16,12},{18,... | collective-permute-start | bytes 1769480 | tf_op jit(solution)/shard_map/ppermute | solution.py:31
  74.8 179.0 %all-gather.18.cloned.1.call-start = ((), (), s32[]{:S(2)}) async-start(), calls=%async_computation.18 | async-start | bytes 2359296 | tf_op jit(solution)/shard_map/all_gather | solution.py:164
  75.9 29.6 %collective-permute-start.2 = (bf16[192,3072]{1,0:T(8,128)(2,1)}, bf16[192,3072]{1,0:T(8,128)(2,1)S(1)}, u32[]{:S(2)}, u32[]{:S(2)}) collective-permute-start(bf16[192,3072]{1,0:T(8,128)(2,1)} %pad_maximum_fusion.2), channel_id=1, source_target_pairs={{0,24},{2,26},{4,28},{6,30},{8,0},{10,2},{12,4},{14,6},{16,8},{18,... | collective-permute-start | bytes 3538952 | tf_op jit(solution)/shard_map/ppermute | solution.py:31
  79.6 188.2 %all-gather.12.cloned.1.call-start = ((), (), s32[]{:S(2)}) async-start(), calls=%async_computation.8 | async-start | bytes 1253376 | tf_op jit(solution)/shard_map/all_gather | solution.py:140
  107.1 111.6 %collective-permute-start.3 = (bf16[384,3072]{1,0:T(8,128)(2,1)}, bf16[384,3072]{1,0:T(8,128)(2,1)}, u32[]{:S(2)}, u32[]{:S(2)}) collective-permute-start(bf16[384,3072]{1,0:T(8,128)(2,1)} %pad_maximum_fusion), channel_id=1, source_target_pairs={{0,16},{2,18},{4,20},{6,22},{8,24},{10,26},{12,28},{14,30},{16,0},... | collective-permute-start | bytes 7077896 | tf_op jit(solution)/shard_map/ppermute | solution.py:31
  109.2 183.6 %all-gather.14.cloned.1.call-start = ((), (), s32[]{:S(2)}) async-start(), calls=%async_computation.9 | async-start | bytes 5013504 | tf_op jit(solution)/shard_map/all_gather | solution.py:142
  112.0 111.7 %copy-start.34 = (s32[1,1024]{1,0:T(1,128)S(1)}, s32[1,1024]{1,0:T(1,128)}, u32[]{:S(2)}) copy-start(s32[1,1024]{1,0:T(1,128)} %param.12) | copy-start | bytes 12292
  222.9 107.3 %all-gather.16.cloned.1.call-start = ((), (), s32[]{:S(2)}) async-start(), calls=%async_computation.10 | async-start | bytes 5013504 | tf_op jit(solution)/shard_map/all_gather | solution.py:183
  223.4 203.1 %reduce-scatter.12.cloned.1.call-start = ((), (), s32[]{:S(2)}) async-start(), calls=%async_computation.12 | async-start | bytes 2359296 | tf_op jit(solution)/shard_map/reduce_scatter | solution.py:222
  225.4 4.3 copy-start.17
  230.0 12.2 %copy-start.5 = (bf16[512,768]{0,1:T(8,128)(2,1)}, bf16[512,768]{0,1:T(8,128)(2,1)S(1)}, u32[]{:S(2)}) copy-start(bf16[512,768]{0,1:T(8,128)(2,1)S(1)} %copy.36) | copy-start | bytes 2359300
  232.0 10.2 %copy-start.3 = (bf16[1024,768]{0,1:T(8,128)(2,1)}, bf16[1024,768]{0,1:T(8,128)(2,1)S(1)}, u32[]{:S(2)}) copy-start(bf16[1024,768]{0,1:T(8,128)(2,1)S(1)} %copy.37) | copy-start | bytes 4718596
  255.5 12.3 %copy-start.18 = (f32[512,768]{1,0:T(8,128)S(1)}, f32[512,768]{1,0:T(8,128)}, u32[]{:S(2)}) copy-start(f32[512,768]{1,0:T(8,128)} %convert_add_fusion) | copy-start | bytes 4718596
  255.5 12.3 %copy-start.33 = (f32[768]{0:T(1024)S(1)}, f32[768]{0:T(1024)}, u32[]{:S(2)}) copy-start(f32[768]{0:T(1024)} %get-tuple-element.72) | copy-start | bytes 9220
  267.8 3.6 copy-start.31
  271.4 21.4 %copy-start.32 = (f32[768]{0:T(1024)S(1)}, f32[768]{0:T(1024)}, u32[]{:S(2)}) copy-start(f32[768]{0:T(1024)} %get-tuple-element.69) | copy-start | bytes 9220
  292.9 7.1 copy-start.9
  292.9 11.7 %copy-start.38 = (f32[512,3072]{1,0:T(8,128)S(1)}, f32[512,3072]{1,0:T(8,128)}, u32[]{:S(2)}) copy-start(f32[512,3072]{1,0:T(8,128)} %get-tuple-element.109) | copy-start | bytes 18874372
  299.6 5.0 copy-start.37
  300.7 4.6 copy-start.35
  330.1 7.4 copy-start.13
  356.2 70.3 %reduce-scatter.10.cloned.1.call-start = ((), (), s32[]{:S(2)}) async-start(), calls=%async_computation.11 | async-start | bytes 2359296 | tf_op jit(solution)/shard_map/reduce_scatter | solution.py:219
  377.0 16.9 %copy-start.6 = (bf16[512,768]{0,1:T(8,128)(2,1)S(1)}, bf16[512,768]{0,1:T(8,128)(2,1)}, u32[]{:S(2)}) copy-start(bf16[512,768]{0,1:T(8,128)(2,1)} %copy-done.5) | copy-start | bytes 2359300
  393.9 5.1 copy-start.2
  393.9 5.1 copy-start.23
  399.0 3.2 copy-start.14
  399.0 86.6 %reduce-scatter.16.cloned.1.call-start = ((), (), s32[]{:S(2)}) async-start(), calls=%async_computation.14 | async-start | bytes 1253376 | tf_op jit(solution)/shard_map/reduce_scatter | solution.py:270
  402.2 161.7 %reduce-scatter.18.cloned.1.call-start = ((), (), s32[]{:S(2)}) async-start(), calls=%async_computation.15 | async-start | bytes 5013504 | tf_op jit(solution)/shard_map/reduce_scatter | solution.py:273
  409.1 233.7 %reduce-scatter.20.cloned.1.call-start = ((), (), s32[]{:S(2)}) async-start(), calls=%async_computation.16 | async-start | bytes 5013504 | tf_op jit(solution)/shard_map/reduce_scatter | solution.py:276
  416.5 297.1 %reduce-scatter.14.cloned.1.call-start = ((), (), s32[]{:S(2)}) async-start(), calls=%async_computation.13 | async-start | bytes 3760128 | tf_op jit(solution)/shard_map/reduce_scatter | solution.py:267
  426.5 6.3 copy-start.16
  432.5 337.7 %reduce-scatter.22.cloned.1.call-start = ((), (), s32[]{:S(2)}) async-start(), calls=%async_computation.20 | async-start | bytes 208896
  434.8 5.0 copy-start.27
  439.7 336.2 %copy-start.25 = (f32[48,15]{0,1:T(8,128)S(1)}, f32[48,15]{0,1:T(8,128)}, u32[]{:S(2)}) copy-start(f32[48,15]{0,1:T(8,128)} %param.17) | copy-start | bytes 8644
  439.7 336.1 %copy-start.28 = (f32[48,15]{0,1:T(8,128)S(1)}, f32[48,15]{0,1:T(8,128)}, u32[]{:S(2)}) copy-start(f32[48,15]{0,1:T(8,128)} %param.19) | copy-start | bytes 8644
  439.7 336.1 %copy-start.29 = (f32[48,15]{0,1:T(8,128)S(1)}, f32[48,15]{0,1:T(8,128)}, u32[]{:S(2)}) copy-start(f32[48,15]{0,1:T(8,128)} %param.18) | copy-start | bytes 8644
  439.8 368.7 %copy-start.8 = (f32[48,9216]{1,0:T(8,128)S(1)}, f32[48,9216]{1,0:T(8,128)}, u32[]{:S(2)}) copy-start(f32[48,9216]{1,0:T(8,128)} %param.14) | copy-start | bytes 5308420
  441.4 367.0 %all-reduce.2.cloned.1.call-start = ((), (), s32[]{:S(2)}) async-start(), calls=%async_computation.17 | async-start | bytes 1769472 | tf_op jit(solution)/shard_map/psum | solution.py:285
  776.5 37.7 %copy-start.30 = (f32[48,15]{0,1:T(8,128)}, f32[48,15]{0,1:T(8,128)S(1)}, u32[]{:S(2)}) copy-start(f32[48,15]{0,1:T(8,128)S(1)} %get-tuple-element.78) | copy-start | bytes 8644
  776.5 37.7 %copy-start.1 = (s32[1,1024]{1,0:T(1,128)S(1)}, s32[1,1024]{1,0:T(1,128)}, u32[]{:S(2)}) copy-start(s32[1,1024]{1,0:T(1,128)} %param.11) | copy-start | bytes 12292
  (9 other events, 13.0 us)
Sparse Core Ops, SparseCore 0:
  10.9 57.8 all-gather.9
  74.9 28.3 all-gather.19
  105.4 27.2 all-gather.17
  135.4 84.7 all-gather.11
  223.0 52.9 all-gather.13
  278.2 51.9 all-gather.15
  356.3 24.6 reduce-scatter.11
  399.1 24.6 reduce-scatter.9
  427.4 58.1 reduce-scatter.15
  489.3 74.5 reduce-scatter.17
  568.2 74.5 reduce-scatter.19
  646.5 67.0 reduce-scatter.13
  717.7 52.4 reduce-scatter.21
  772.9 35.4 all-reduce.1
